TPU v7x, 128 devices: a whole 4x4x4 slice. The times are simulated.
128 devices in a mesh: dp: 32 (over x_hi, y, z), tensor: 4 (over x_lo, core).
Axes of the slice: x: 4 (x_hi: 2, x_lo: 2; x = x_hi * 2 + x_lo), y: 4, z: 4, core: 2. Of those that a mesh axis runs over, the one named last changes fastest.
Arguments:
- inputs: bfloat16 [32768, 640], P('dp'), may hold values from -6 to 6
- segments: int32 [32768], P('dp'), may hold values from 0 to 63, never falling along the last dimension, each value on 1 to 2048 neighbouring positions
- positions: int32 [32768], P('dp'), may hold values from 0 to 2047
- cotangent: bfloat16 [32768, 640], P('dp'), may hold values from -6 to 6
- w_query: bfloat16 [640, 1024], P(None, 'tensor'), may hold values from -0.25 to 0.25
- w_key: bfloat16 [640, 256], replicated, may hold values from -0.25 to 0.25
- w_value: bfloat16 [640, 256], replicated, may hold values from -0.25 to 0.25
- w_out: bfloat16 [1024, 640], P('tensor'), may hold values from -0.1875 to 0.1875
- w_gate: bfloat16 [640, 2048], P(None, 'tensor'), may hold values from -0.25 to 0.25
- w_up: bfloat16 [640, 2048], P(None, 'tensor'), may hold values from -0.25 to 0.25
- w_down: bfloat16 [2048, 640], P('tensor'), may hold values from -0.125 to 0.125
- g_attn_in: float32 [640], replicated, may hold values from 0.1 to 1.9
- g_attn_out: float32 [640], replicated, may hold values from 0.1 to 1.9
- g_ffn_in: float32 [640], replicated, may hold values from 0.1 to 1.9
- g_ffn_out: float32 [640], replicated, may hold values from 0.1 to 1.9
- g_query: float32 [256], replicated, may hold values from 0.1 to 1.9
- g_key: float32 [256], replicated, may hold values from 0.1 to 1.9
Outputs:
- output: bfloat16 [32768, 640], P('dp')
- input_grad: bfloat16 [32768, 640], P('dp')
- grad_query: float32 [640, 1024], P(None, 'tensor')
- grad_key: float32 [640, 256], replicated
- grad_value: float32 [640, 256], replicated
- grad_out: float32 [1024, 640], P('tensor')
- grad_gate: float32 [640, 2048], P(None, 'tensor')
- grad_up: float32 [640, 2048], P(None, 'tensor')
- grad_down: float32 [2048, 640], P('tensor')
- grad_attn_in: float32 [640], replicated
- grad_attn_out: float32 [640], replicated
- grad_ffn_in: float32 [640], replicated
- grad_ffn_out: float32 [640], replicated
- grad_qnorm: float32 [256], replicated
- grad_knorm: float32 [256], replicated
Inputs may be any that keep to these rules, and one draw needn't show every extreme that they name: `segments`: document numbers never fall along the tokens; a document holds at most 2048 tokens.
All inputs are finite; a program needn't handle non-finite values.
Results may differ from a plain program's by a relative error of at most 0.03.
Values may be sent and summed in bfloat16 or wider, within the bound.
A program may use at most 128 MiB of HBM per device.

v0:
```python
import math
import jax
import jax.numpy as jnp
from jax import lax
from jax.sharding import PartitionSpec as P

WINDOW = 512
LENGTH = 1024
EPSILON = 1e-06
ROPE_BASE = 10000.0
NEG_LARGE = -1e30


def in_blocks(x, dim, size):
    before, after = (x.shape[:dim], x.shape[dim + 1 :])
    return jnp.moveaxis(x.reshape(*before, size, -1, *after), dim, 0)


def sum_at_owner(x, axis, dim):
    size = lax.axis_size(axis)
    tiles = lax.all_to_all(in_blocks(x, dim, size), axis, 0, 0, tiled=True)
    return jnp.sum(tiles.astype(jnp.float32), axis=0)


def in_order(tiles, dim):
    tiles = jnp.moveaxis(tiles, 0, dim)
    lengths = tiles.shape
    return tiles.reshape(*lengths[:dim], lengths[dim] * lengths[dim + 1], *lengths[dim + 2 :])


def copy_for_each(x, axis):
    copies = jnp.broadcast_to(x, (lax.axis_size(axis), *x.shape))
    return lax.all_to_all(copies, axis, split_axis=0, concat_axis=0, tiled=True)


def collect(x, axis, dim):
    return in_order(copy_for_each(x, axis), dim)


def in_one_piece(arrays, axis, dim, along):
    both = jnp.concatenate(arrays, axis=along)
    out, at, gathered = (lax.all_gather(both, axis, axis=dim, tiled=True), 0, [])
    for a in arrays:
        gathered.append(lax.slice_in_dim(out, at, at + a.shape[along], axis=along))
        at += a.shape[along]
    return tuple(gathered)


def rms_scale(values, gain_vec):
    return (
        values * lax.rsqrt(jnp.mean(values * values, axis=-1, keepdims=True) + EPSILON) * gain_vec
    )


def gain_term(values, grad_vec):
    scaled = values * lax.rsqrt(jnp.mean(values * values, axis=-1, keepdims=True) + EPSILON)
    return jnp.sum(grad_vec * scaled, axis=0)


def rope_tables(positions, head_size):
    half_size = head_size // 2
    inv_freq = ROPE_BASE ** (-2.0 * jnp.arange(half_size, dtype=jnp.float32) / head_size)
    angles = positions.astype(jnp.float32)[:, None] * inv_freq[None, :]
    return (jnp.cos(angles), jnp.sin(angles))


def rotate(values, cosine, sine_table):
    half_size = values.shape[-1] // 2
    first_half = values[..., :half_size]
    second_half = values[..., half_size:]
    return jnp.concatenate(
        [
            first_half * cosine - second_half * sine_table,
            second_half * cosine + first_half * sine_table,
        ],
        axis=-1,
    )


def rotary_norm(raw_vec, gain_vec, cosine, sine_table):
    return rotate(rms_scale(raw_vec, gain_vec), cosine, sine_table)


def windows(blocks, fill_value):
    earlier = jnp.concatenate([jnp.full_like(blocks[:, :1], fill_value), blocks[:, :-1]], axis=1)
    return jnp.concatenate([earlier, blocks], axis=2)


def unwindow(grads, width):
    front_half = grads[:, :, :width]
    back_half = grads[:, :, width:]
    shifted = jnp.concatenate([front_half[:, 1:], jnp.zeros_like(front_half[:, :1])], axis=1)
    return back_half + shifted


def allowed_mask(seg_rows, seg_keys, width):
    row_ids = lax.broadcasted_iota(jnp.int32, (width, 2 * width), 0)
    key_ids = lax.broadcasted_iota(jnp.int32, (width, 2 * width), 1)
    in_window = (key_ids > row_ids) & (key_ids <= row_ids + width)
    return in_window & (seg_rows[:, None] == seg_keys[None, :])


def block_forward(block_item, score_scale):
    q_block, k_window, v_window, seg_rows, seg_keys = block_item
    width = q_block.shape[1]
    scores = (
        jnp.einsum("hqd,kd->hqk", q_block, k_window, preferred_element_type=jnp.float32)
        * score_scale
    )
    allowed = allowed_mask(seg_rows, seg_keys, width)[None]
    masked = jnp.where(allowed, scores, NEG_LARGE)
    row_max = jnp.max(masked, axis=-1, keepdims=True)
    expo_terms = jnp.where(allowed, jnp.exp(masked - row_max), 0.0)
    row_total = jnp.sum(expo_terms, axis=-1, keepdims=True)
    prob_low = (expo_terms / row_total).astype(jnp.bfloat16)
    block_out = jnp.einsum("hqk,kd->hqd", prob_low, v_window, preferred_element_type=jnp.float32)
    return (block_out, (row_max + jnp.log(row_total))[..., 0])


def block_backward(block_item, score_scale):
    q_block, k_window, v_window, seg_rows, seg_keys, log_totals, grad_block = block_item
    width = q_block.shape[1]
    scores = (
        jnp.einsum("hqd,kd->hqk", q_block, k_window, preferred_element_type=jnp.float32)
        * score_scale
    )
    allowed = allowed_mask(seg_rows, seg_keys, width)[None]
    prob_full = jnp.where(allowed, jnp.exp(scores - log_totals[..., None]), 0.0)
    grad_prob = jnp.einsum("hqd,kd->hqk", grad_block, v_window, preferred_element_type=jnp.float32)
    row_dot = jnp.sum(prob_full * grad_prob, axis=-1, keepdims=True)
    grad_scores = (prob_full * (grad_prob - row_dot)).astype(jnp.bfloat16)
    grad_q = (
        jnp.einsum("hqk,kd->hqd", grad_scores, k_window, preferred_element_type=jnp.float32)
        * score_scale
    )
    grad_k = (
        jnp.einsum("hqk,hqd->kd", grad_scores, q_block, preferred_element_type=jnp.float32)
        * score_scale
    )
    grad_v = jnp.einsum(
        "hqk,hqd->kd",
        prob_full.astype(jnp.bfloat16),
        grad_block,
        preferred_element_type=jnp.float32,
    )
    return (grad_q, grad_k, grad_v)


def local(
    inputs,
    segments,
    positions,
    cotangent,
    w_query,
    w_key,
    w_value,
    w_out,
    w_gate,
    w_up,
    w_down,
    g_attn_in,
    g_attn_out,
    g_ffn_in,
    g_ffn_out,
    g_query,
    g_key,
):
    row_count = inputs.shape[0]
    head_size = w_key.shape[1]
    heads_here = w_query.shape[1] // head_size
    seqs_here = row_count // LENGTH
    blocks_per = LENGTH // WINDOW
    block_total = seqs_here * blocks_per
    score_scale = 1.0 / math.sqrt(head_size)
    share_rows = row_count // lax.axis_size("tensor")
    first_row = lax.axis_index("tensor") * share_rows

    def my_rows(values):
        return lax.dynamic_slice_in_dim(values, first_row, share_rows, 0)

    whole_x = inputs.astype(jnp.float32)
    normed = rms_scale(whole_x, g_attn_in).astype(jnp.bfloat16)
    query_raw = jnp.dot(normed, w_query, preferred_element_type=jnp.float32)
    key_raw = jnp.dot(normed, w_key, preferred_element_type=jnp.float32)
    value_raw = jnp.dot(normed, w_value, preferred_element_type=jnp.float32)
    cosine, sine_table = rope_tables(positions, head_size)
    query_heads = query_raw.reshape(row_count, heads_here, head_size).transpose(1, 0, 2)
    q_rot, q_pull = jax.vjp(
        lambda raw_vec, gain_vec: rotary_norm(raw_vec, gain_vec, cosine, sine_table),
        query_heads,
        g_query,
    )
    k_rot, k_pull = jax.vjp(
        lambda raw_vec, gain_vec: rotary_norm(raw_vec, gain_vec, cosine, sine_table), key_raw, g_key
    )
    q_blocks = (
        q_rot.astype(jnp.bfloat16)
        .reshape(heads_here, block_total, WINDOW, head_size)
        .transpose(1, 0, 2, 3)
    )
    k_windows = windows(
        k_rot.astype(jnp.bfloat16).reshape(seqs_here, blocks_per, WINDOW, head_size), 0
    ).reshape(block_total, 2 * WINDOW, head_size)
    v_windows = windows(
        value_raw.astype(jnp.bfloat16).reshape(seqs_here, blocks_per, WINDOW, head_size), 0
    ).reshape(block_total, 2 * WINDOW, head_size)
    seg_rows = segments.reshape(block_total, WINDOW)
    seg_keys = windows(segments.reshape(seqs_here, blocks_per, WINDOW), -1).reshape(
        block_total, 2 * WINDOW
    )
    block_items = (q_blocks, k_windows, v_windows, seg_rows, seg_keys)
    heads_out, log_totals = lax.map(
        lambda block_item: block_forward(block_item, score_scale), block_items
    )
    heads_low = (
        heads_out.astype(jnp.bfloat16)
        .transpose(0, 2, 1, 3)
        .reshape(row_count, heads_here * head_size)
    )
    attn_term = jnp.dot(heads_low, w_out, preferred_element_type=jnp.float32)
    attn_sum = sum_at_owner(attn_term.astype(jnp.bfloat16), "tensor", 0)
    x_rows = my_rows(whole_x)
    attn_norm, attn_pull = jax.vjp(lambda values: rms_scale(values, g_attn_out), attn_sum)
    mid_rows = x_rows + attn_norm
    ffn_in, ffn_pull = jax.vjp(lambda values: rms_scale(values, g_ffn_in), mid_rows)
    ffn_low = collect(ffn_in.astype(jnp.bfloat16), "tensor", 0)
    gate_raw = jnp.dot(ffn_low, w_gate, preferred_element_type=jnp.float32)
    up_raw = jnp.dot(ffn_low, w_up, preferred_element_type=jnp.float32)
    hidden_full, act_pull = jax.vjp(
        lambda gate_in, up_in: jax.nn.gelu(gate_in, approximate=True) * up_in, gate_raw, up_raw
    )
    hidden = hidden_full.astype(jnp.bfloat16)
    ffn_term = jnp.dot(hidden, w_down, preferred_element_type=jnp.float32)
    ffn_sum = sum_at_owner(ffn_term.astype(jnp.bfloat16), "tensor", 0)
    cot_rows = my_rows(cotangent).astype(jnp.float32)
    out_norm, out_pull = jax.vjp(lambda values: rms_scale(values, g_ffn_out), ffn_sum)
    result = mid_rows + out_norm
    grad_ffn = out_pull(cot_rows)[0]
    output, grad_ffn_low = in_one_piece(
        (result.astype(jnp.bfloat16), grad_ffn.astype(jnp.bfloat16)), "tensor", 0, 1
    )
    grad_hidden = jnp.einsum("rd,fd->rf", grad_ffn_low, w_down, preferred_element_type=jnp.float32)
    grad_down = jnp.einsum("rf,rd->fd", hidden, grad_ffn_low, preferred_element_type=jnp.float32)
    grad_gate_full, grad_up_full = act_pull(grad_hidden)
    grad_gate_low = grad_gate_full.astype(jnp.bfloat16)
    grad_up_low = grad_up_full.astype(jnp.bfloat16)
    grad_gate = jnp.einsum("rd,rf->df", ffn_low, grad_gate_low, preferred_element_type=jnp.float32)
    grad_up = jnp.einsum("rd,rf->df", ffn_low, grad_up_low, preferred_element_type=jnp.float32)
    ffn_in_term = jnp.einsum(
        "rf,df->rd", grad_gate_low, w_gate, preferred_element_type=jnp.float32
    ) + jnp.einsum("rf,df->rd", grad_up_low, w_up, preferred_element_type=jnp.float32)
    ffn_in_grad = sum_at_owner(ffn_in_term.astype(jnp.bfloat16), "tensor", 0)
    grad_mid = cot_rows + ffn_pull(ffn_in_grad)[0]
    grad_attn = attn_pull(grad_mid)[0]
    grad_attn_low = collect(grad_attn.astype(jnp.bfloat16), "tensor", 0)
    grad_out = jnp.einsum("rh,rd->hd", heads_low, grad_attn_low, preferred_element_type=jnp.float32)
    grad_heads = jnp.einsum(
        "rd,hd->rh", grad_attn_low, w_out, preferred_element_type=jnp.float32
    ).astype(jnp.bfloat16)
    grad_blocks = grad_heads.reshape(block_total, WINDOW, heads_here, head_size).transpose(
        0, 2, 1, 3
    )
    grad_qb, grad_kw, grad_vw = lax.map(
        lambda block_item: block_backward(block_item, score_scale),
        block_items + (log_totals, grad_blocks),
    )
    grad_q_rot = grad_qb.transpose(1, 0, 2, 3).reshape(heads_here, row_count, head_size)
    grad_k_rot = unwindow(
        grad_kw.reshape(seqs_here, blocks_per, 2 * WINDOW, head_size), WINDOW
    ).reshape(row_count, head_size)
    grad_v_full = unwindow(
        grad_vw.reshape(seqs_here, blocks_per, 2 * WINDOW, head_size), WINDOW
    ).reshape(row_count, head_size)
    grad_query_raw, grad_qnorm = q_pull(grad_q_rot)
    grad_key_raw, grad_knorm = k_pull(grad_k_rot)
    grad_q_low = (
        grad_query_raw.transpose(1, 0, 2)
        .reshape(row_count, heads_here * head_size)
        .astype(jnp.bfloat16)
    )
    grad_k_low = grad_key_raw.astype(jnp.bfloat16)
    grad_v_low = grad_v_full.astype(jnp.bfloat16)
    grad_query = jnp.einsum("rd,rh->dh", normed, grad_q_low, preferred_element_type=jnp.float32)
    grad_key = jnp.einsum("rd,rh->dh", normed, grad_k_low, preferred_element_type=jnp.float32)
    grad_value = jnp.einsum("rd,rh->dh", normed, grad_v_low, preferred_element_type=jnp.float32)
    input_term = jnp.einsum("rh,dh->rd", grad_q_low, w_query, preferred_element_type=jnp.float32)
    input_term = input_term + jnp.einsum(
        "rh,dh->rd", grad_k_low, w_key, preferred_element_type=jnp.float32
    )
    input_term = input_term + jnp.einsum(
        "rh,dh->rd", grad_v_low, w_value, preferred_element_type=jnp.float32
    )
    input_sum = sum_at_owner(input_term.astype(jnp.bfloat16), "tensor", 0)
    x_grad_norm = jax.vjp(lambda values: rms_scale(values, g_attn_in), x_rows)[1](input_sum)[0]
    grad_rows = grad_mid + x_grad_norm
    gain_inputs = (x_rows, input_sum, attn_sum, grad_mid, mid_rows, ffn_in_grad, ffn_sum, cot_rows)
    input_grad = collect(grad_rows.astype(jnp.bfloat16), "tensor", 0)
    grad_attn_in = gain_term(gain_inputs[0], gain_inputs[1])
    grad_attn_out = gain_term(gain_inputs[2], gain_inputs[3])
    grad_ffn_in = gain_term(gain_inputs[4], gain_inputs[5])
    grad_ffn_out = gain_term(gain_inputs[6], gain_inputs[7])
    grad_query, grad_out, grad_gate, grad_up, grad_down = (
        lax.psum(grad_query.astype(jnp.bfloat16), "dp").astype(jnp.float32),
        lax.psum(grad_out.astype(jnp.bfloat16), "dp").astype(jnp.float32),
        lax.psum(grad_gate.astype(jnp.bfloat16), "dp").astype(jnp.float32),
        lax.psum(grad_up.astype(jnp.bfloat16), "dp").astype(jnp.float32),
        lax.psum(grad_down.astype(jnp.bfloat16), "dp").astype(jnp.float32),
    )
    summed_all = lax.psum(
        (
            grad_key,
            grad_value,
            grad_attn_in,
            grad_attn_out,
            grad_ffn_in,
            grad_ffn_out,
            grad_qnorm,
            grad_knorm,
        ),
        ("dp", "tensor"),
    )
    return (
        output,
        input_grad,
        grad_query,
        summed_all[0],
        summed_all[1],
        grad_out,
        grad_gate,
        grad_up,
        grad_down,
        summed_all[2],
        summed_all[3],
        summed_all[4],
        summed_all[5],
        summed_all[6],
        summed_all[7],
    )


def solution(mesh):
    placed = (
        P("dp", None),
        P("dp"),
        P("dp"),
        P("dp", None),
        P(None, "tensor"),
        P(),
        P(),
        P("tensor", None),
        P(None, "tensor"),
        P(None, "tensor"),
        P("tensor", None),
        P(),
        P(),
        P(),
        P(),
        P(),
        P(),
    )
    return jax.shard_map(
        local,
        mesh=mesh,
        in_specs=placed,
        out_specs=(
            P("dp", None),
            P("dp", None),
            P(None, "tensor"),
            P(),
            P(),
            P("tensor", None),
            P(None, "tensor"),
            P(None, "tensor"),
            P("tensor", None),
            P(),
            P(),
            P(),
            P(),
            P(),
            P(),
        ),
        check_vma=False,
    )
```

profile of v0, /device:TPU:1, one launch (start us, length us, event | category | flops | bytes accessed | tf_op | source)
XLA Modules:
  0.0 761.8 jit_solution(5090513711252032929)
XLA Ops:
  9.4 1.6 multiply_reduce_fusion.1
  11.1 2.1 convolution_convert_fusion.6
  15.2 2.4 fusion.97
  17.9 2.4 fusion.91
  22.3 10.3 %while.28 = (s32[]{:T(128)}, bf16[2,1,512,256]{3,2,1,0:T(8,128)(2,1)S(1)}, f32[2,1,512]{2,1,0:T(1,128)}, s32[2,512]{1,0:T(2,128)S(1)}, s32[2,1024]{1,0:T(2,128)S...) while((s32[]{:T(128)}, ...), condition=%wide.region_6.7_spmd.clone, body=%wide.region_3.6_spmd.sunk.clone | while | flops 552075264 | bytes 8220833 | solution.py:212
  22.3 2.0 fusion.189
  25.3 1.4 fusion.191
  27.5 2.0 fusion.189
  30.5 1.4 fusion.191
  32.6 2.6 convolution_convert_fusion
  35.2 5.7 all-to-all-start
  40.9 1.6 convert_element_type.144
  42.5 14.9 %all-to-all-done = bf16[4,256,640]{2,1,0:T(8,128)(2,1)} async-done(((bf16[4,256,640]{2,1,0:T(8,128)(2,1)}), bf16[4,256,640]{2,1,0:T(8,128)(2,1)}, u32[]{:S(2)}, u32[]{:S(2)}) %all-to-all-start) | async-done | bytes 1310752 | tf_op jit(solution)/shard_map/all_to_all | solution.py:21
  57.4 1.6 convert_reduce_fusion.3
  59.6 2.0 multiply_reduce_fusion.14
  62.4 19.7 %all_to_all.35 = bf16[4,256,640]{2,1,0:T(8,128)(2,1)S(1)} all-to-all(bf16[4,256,640]{2,1,0:T(8,128)(2,1)S(1)} %broadcast_in_dim.57), channel_id=1, replica_groups=mesh['dp'=32,'tensor'=4] {'tensor'}, dimensions={0} | all-to-all | bytes 2621440 | tf_op jit(solution)/shard_map/all_to_all | solution.py:33
  83.7 2.6 multiply_convert_fusion.3
  87.3 19.8 %all_to_all.36 = bf16[4,256,640]{2,1,0:T(8,128)(2,1)S(1)} all-to-all(bf16[4,256,640]{2,1,0:T(8,128)(2,1)S(1)} %bitcast.223), channel_id=1, replica_groups=mesh['dp'=32,'tensor'=4] {'tensor'}, dimensions={0} | all-to-all | bytes 2621440 | tf_op jit(solution)/shard_map/all_to_all | solution.py:21
  109.6 36.9 %all-gather.2.cloned.1.call-done = bf16[1024,1280]{1,0:T(8,128)(2,1)} async-done(((bf16[256,1280]{1,0:T(8,128)(2,1)}), bf16[1024,1280]{1,0:T(8,128)(2,1)}) %all-gather.2.cloned.1.call-update) | async-done | bytes 2621456 | tf_op jit(solution)/shard_map/all_gather | solution.py:42
  146.5 5.0 multiply_convert_fusion.2
  154.2 18.6 %all_to_all.37 = bf16[4,256,640]{2,1,0:T(8,128)(2,1)S(1)} all-to-all(bf16[4,256,640]{2,1,0:T(8,128)(2,1)S(1)} %bitcast.209), channel_id=1, replica_groups=mesh['dp'=32,'tensor'=4] {'tensor'}, dimensions={0} | all-to-all | bytes 2621440 | tf_op jit(solution)/shard_map/all_to_all | solution.py:21
  173.9 2.0 multiply_reduce_fusion.7
  177.3 5.3 all-to-all-start.4
  182.6 3.0 convolution_convert_fusion.3
  185.6 1.7 convolution_convert_fusion.4
  187.9 1.9 convolution_convert_fusion.2
  189.8 9.4 %all-to-all-done.4 = bf16[4,256,640]{2,1,0:T(8,128)(2,1)} async-done(((bf16[4,256,640]{2,1,0:T(8,128)(2,1)}), bf16[4,256,640]{2,1,0:T(8,128)(2,1)}, u32[]{:S(2)}, u32[]{:S(2)}) %all-to-all-start.4) | async-done | bytes 1310752 | tf_op jit(solution)/shard_map/all_to_all | solution.py:33
  199.1 2.7 convolution_convert_fusion.7
  201.9 2.0 convolution_convert_fusion.5
  203.9 15.6 %while.29 = (s32[]{:T(128)}, f32[2,1,512,256]{3,2,1,0:T(8,128)S(1)}, f32[2,1024,256]{2,1,0:T(8,128)}, f32[2,1024,256]{2,1,0:T(8,128)}, s32[2,512]{1,0:T(2,128)S(...) while((s32[]{:T(128)}, ...), condition=%wide.region_18.19_spmd.clone, body=%wide.region_16.18_spmd.sunk.clone | while | flops 1349910528 | bytes 58758412 | solution.py:263
  219.5 2.3 fusion.94
  223.5 1.5 convolution_convert_fusion.8
  225.1 1.8 fusion.118
  229.2 2.3 fusion.100
  233.1 2.1 fusion.119
  236.3 3.5 add_convert_fusion
  239.8 5.4 all-to-all-start.5
  245.2 18.8 %all-to-all-done.5 = bf16[4,256,640]{2,1,0:T(8,128)(2,1)} async-done(((bf16[4,256,640]{2,1,0:T(8,128)(2,1)}), bf16[4,256,640]{2,1,0:T(8,128)(2,1)}, u32[]{:S(2)}, u32[]{:S(2)}) %all-to-all-start.5) | async-done | bytes 1310752 | tf_op jit(solution)/shard_map/all_to_all | solution.py:21
  264.1 1.6 convert_reduce_fusion
  267.4 4.1 all-to-all-start.6
  271.5 2.7 fusion.113
  274.2 1.6 fusion.112
  275.8 2.5 slice.62
  278.3 71.3 %all-reduce.9 = (f32[640]{0:T(1024)}, f32[640]{0:T(1024)}, f32[640]{0:T(1024)}, f32[640]{0:T(1024)}, f32[256]{0:T(256)}, /*index=5*/f32[256]{0:T(256)}) all-reduce(f32[640]{0:T(1024)S(1)} %get-tuple-element.133, f32[640]{0:T(1024)S(1)} %copy-done.65, f32[640]{0:T(1024)S(1)} %copy-done.64, ...), channel_id=1, replica_groups=mesh['dp'=32,'tensor'=4] {'dp','tensor'}, use_global_device_ids=true, to_apply=%region_32.33 | all-reduce | flops 3072 | bytes 24576 | tf_op jit(solution)/shard_map/psum | solution.py:309
  349.6 226.8 %all-reduce.17.cloned.1.call-done = (bf16[640,256]{1,0:T(8,128)(2,1)}, bf16[256,640]{1,0:T(8,128)(2,1)}, bf16[640,512]{1,0:T(8,128)(2,1)}, bf16[640,512]{1,0:T(8,128)(2,1)}, bf16[512,640]{1,0:T(8,128)(2,1)}) async-done(((bf16[640,256]{1,0:T(8,128)(2,1)}, bf16[256,640]{1,0:T(8,128)(2,1)}, bf16[640,512]{1,0:T(8,128)(2,1)}, bf16[640,512]{1,0:T(8,128)(2,1)}, bf16[512,640]{1,0:T(8,128)(2,1)}), ...) | async-done | bytes 2621456 | tf_op jit(solution)/shard_map/psum | solution.py:303
  576.4 2.0 convert_element_type.173
  578.4 1.9 convert_element_type.175
  583.8 168.3 %all-reduce.15.cloned.1.call-done = (f32[640,256]{1,0:T(8,128)}, f32[640,256]{1,0:T(8,128)}) async-done(((f32[640,256]{1,0:T(8,128)}, f32[640,256]{1,0:T(8,128)}), (f32[640,256]{1,0:T(8,128)}, f32[640,256]{1,0:T(8,128)})) %all-reduce.15.cloned.1.call-update) | async-done | bytes 1310736 | tf_op jit(solution)/shard_map/psum | solution.py:309
  (290 shorter events, 51.9 us)
Async XLA Ops:
  7.2 79.1 %copy-start = (bf16[512,640]{1,0:T(8,128)(2,1)S(1)}, bf16[512,640]{1,0:T(8,128)(2,1)}, u32[]{:S(2)}) copy-start(bf16[512,640]{1,0:T(8,128)(2,1)} %param.31) | copy-start | bytes 1966084
  7.2 10.6 %copy-start.79 = (f32[128]{0:T(128)}, f32[128]{0:T(128)S(1)}, u32[]{:S(2)}) copy-start(f32[128]{0:T(128)S(1)} %multiply_power_fusion) | copy-start | bytes 1540
  11.1 3.0 copy-start.81
  14.9 2.7 copy-start.68
  14.9 2.9 copy-start.4
  15.0 2.7 copy-start.70
  15.0 2.6 copy-start.48
  35.2 22.2 %all-to-all-start = ((bf16[4,256,640]{2,1,0:T(8,128)(2,1)}), bf16[4,256,640]{2,1,0:T(8,128)(2,1)}, u32[]{:S(2)}, u32[]{:S(2)}) async-start(bf16[4,256,640]{2,1,0:T(8,128)(2,1)} %bitcast.29), calls=%async_computation | async-start | bytes 2621440 | tf_op jit(solution)/shard_map/all_to_all | solution.py:21
  40.9 105.6 %all-gather.2.cloned.1.call-start = ((), (), s32[]{:S(2)}) async-start(), calls=%async_computation.7 | async-start | bytes 3276800 | tf_op jit(solution)/shard_map/all_gather | solution.py:42
  57.4 4.8 copy-start.50
  62.3 19.8 %copy-start.36 = (bf16[640,512]{1,0:T(8,128)(2,1)S(1)}, bf16[640,512]{1,0:T(8,128)(2,1)}, u32[]{:S(2)}) copy-start(bf16[640,512]{1,0:T(8,128)(2,1)} %param.29) | copy-start | bytes 1966084
  83.7 2.6 copy-start.83
  86.3 20.9 %copy-start.84 = (bf16[1024,512]{1,0:T(8,128)(2,1)}, bf16[1024,512]{1,0:T(8,128)(2,1)S(1)}, u32[]{:S(2)}) copy-start(bf16[1024,512]{1,0:T(8,128)(2,1)S(1)} %get-tuple-element.220) | copy-start | bytes 3145732
  87.3 20.2 %copy-start.29 = (bf16[1024,640]{1,0:T(8,128)(2,1)S(1)}, bf16[1024,640]{1,0:T(8,128)(2,1)}, u32[]{:S(2)}) copy-start(bf16[1024,640]{1,0:T(8,128)(2,1)} %param.24) | copy-start | bytes 3932164
  87.3 20.2 %copy-start.60 = (f32[640]{0:T(1024)S(1)}, f32[640]{0:T(1024)}, u32[]{:S(2)}) copy-start(f32[640]{0:T(1024)} %param.35) | copy-start | bytes 7684
  146.5 5.1 copy-start.37
  154.2 18.9 %copy-start.51 = (f32[640]{0:T(1024)S(1)}, f32[640]{0:T(1024)}, u32[]{:S(2)}) copy-start(f32[640]{0:T(1024)} %param.34) | copy-start | bytes 7684
  154.2 18.9 %copy-start.59 = (f32[256]{0:T(256)S(1)}, f32[256]{0:T(256)}, u32[]{:S(2)}) copy-start(f32[256]{0:T(256)} %copy-done.58) | copy-start | bytes 3076
  173.1 2.9 copy-start.76
  176.1 6.5 copy-start.17
  177.3 21.8 %all-to-all-start.4 = ((bf16[4,256,640]{2,1,0:T(8,128)(2,1)}), bf16[4,256,640]{2,1,0:T(8,128)(2,1)}, u32[]{:S(2)}, u32[]{:S(2)}) async-start(bf16[4,256,640]{2,1,0:T(8,128)(2,1)} %broadcast_in_dim.61), calls=%async_computation.4 | async-start | bytes 2621440 | tf_op jit(solution)/shard_map/all_to_all | solution.py:33
  182.6 393.8 %all-reduce.17.cloned.1.call-start = ((), (), s32[]{:S(2)}) async-start(), calls=%async_computation.9 | async-start | bytes 5242880 | tf_op jit(solution)/shard_map/psum | solution.py:303
  182.6 3.0 copy-start.27
  199.1 2.8 copy-start.41
  199.1 4.7 copy-start.24
  199.1 4.8 copy-start.55
  203.9 15.6 %copy-start.80 = (f32[128]{0:T(128)S(1)}, f32[128]{0:T(128)}, u32[]{:S(2)}) copy-start(f32[128]{0:T(128)} %copy-done.79) | copy-start | bytes 1540
  219.5 2.8 copy-start.69
  225.1 3.0 copy-start.20
  229.0 2.4 copy-start.3
  229.0 2.4 copy-start.47
  229.0 2.4 copy-start.73
  229.1 2.8 copy-start.67
  239.8 5.4 copy-start.74
  239.8 25.9 %copy-start.6 = (f32[1024,640]{1,0:T(8,128)S(1)}, f32[1024,640]{1,0:T(8,128)}, u32[]{:S(2)}) copy-start(f32[1024,640]{1,0:T(8,128)} %convert_element_type.144) | copy-start | bytes 7864324
  239.8 24.3 %all-to-all-start.5 = ((bf16[4,256,640]{2,1,0:T(8,128)(2,1)}), bf16[4,256,640]{2,1,0:T(8,128)(2,1)}, u32[]{:S(2)}, u32[]{:S(2)}) async-start(bf16[4,256,640]{2,1,0:T(8,128)(2,1)} %bitcast.207), calls=%async_computation.5 | async-start | bytes 2621440 | tf_op jit(solution)/shard_map/all_to_all | solution.py:21
  245.2 20.7 %copy-start.8 = (f32[256,640]{1,0:T(8,128)S(1)}, f32[256,640]{1,0:T(8,128)}, u32[]{:S(2)}) copy-start(f32[256,640]{1,0:T(8,128)} %copy-done.7) | copy-start | bytes 1966084
  266.2 5.3 copy-start.11
  267.4 82.3 %all-to-all-start.6 = ((bf16[4,256,640]{2,1,0:T(8,128)(2,1)}), bf16[4,256,640]{2,1,0:T(8,128)(2,1)S(1)}, u32[]{:S(2)}, u32[]{:S(2)}) async-start(bf16[4,256,640]{2,1,0:T(8,128)(2,1)} %broadcast_in_dim.101), calls=%async_computation.6 | async-start | bytes 2621440 | tf_op jit(solution)/shard_map/all_to_all | solution.py:33
  271.5 2.7 copy-start.13
  271.5 480.7 %all-reduce.15.cloned.1.call-start = ((), (), s32[]{:S(2)}) async-start(), calls=%async_computation.8 | async-start | bytes 2621440 | tf_op jit(solution)/shard_map/psum | solution.py:309
  275.7 2.5 copy-start.63
  275.7 2.5 copy-start.64
  275.7 2.5 copy-start.65
  576.4 3.8 copy-start.35
  576.4 5.0 copy-start.34
  580.2 2.5 copy-start.33
  752.1 3.2 copy-start.1
  (52 other events, 76.5 us)
Sparse Core Ops, SparseCore 0:
  109.7 36.6 all-gather.1
  235.4 340.9 all-reduce.16
  581.9 170.1 all-reduce.14
where the time goes:
time: 763 us; the launch traced here: 762 us
  waiting for transfers between devices  475 us (62%)
  blocking collectives  129 us (17%)
  matrix products  55.3 us (7%)
  other arithmetic  39.8 us (5%)
  local copies, waits for them, and re-layouts  26.5 us (3%)
  starting transfers between devices  20.5 us (3%)
  between operations  14.7 us (2%)
    psum x1, waiting for transfers between devices, local(): lax.psum(grad_query.astype(jnp.bfloat16), 'dp').astype(jnp.float32)  227 us
    psum x1, waiting for transfers between devices, local(): lax.psum((grad_key, grad_value, grad_attn_in, grad_attn_out, grad_ffn_in,...  168 us
    psum x1, blocking collectives, local(): lax.psum((grad_key, grad_value, grad_attn_in, grad_attn_out, grad_ffn_in,...  71.3 us
    all_to_all x2, blocking collectives, sum_at_owner(): tiles = lax.all_to_all(in_blocks(x, dim, size), axis, 0, 0, tiled=True)  38.5 us
    all_gather x1, waiting for transfers between devices, in_one_piece(): lax.all_gather(both, axis, axis=dim, tiled=True)  36.9 us
    all_to_all x2, waiting for transfers between devices, sum_at_owner(): tiles = lax.all_to_all(in_blocks(x, dim, size), axis, 0, 0, tiled=True)  33.7 us
    all_to_all x1, blocking collectives, copy_for_each(): return lax.all_to_all(copies, axis, split_axis=0, concat_axis=0, tiled=True)  19.7 us
  transfers between devices with their start and end apart: 7, of which 6 were waited for; matrix products, arithmetic and copies ran while one was open for 4% of the time, Pallas kernels for 0%

commit v1 on v0

--- a/solution.py
+++ b/solution.py
@@ -9,6 +9,12 @@
 EPSILON = 1e-06
 ROPE_BASE = 10000.0
 NEG_LARGE = -1e30
+
+
+def add_all(x, name):
+    parts = lax.all_gather(x, name, axis=0, tiled=False)
+    total = parts.sum(axis=0)
+    return total
 
 
 def in_blocks(x, dim, size):
@@ -300,7 +306,7 @@
     grad_ffn_in = gain_term(gain_inputs[4], gain_inputs[5])
     grad_ffn_out = gain_term(gain_inputs[6], gain_inputs[7])
     grad_query, grad_out, grad_gate, grad_up, grad_down = (
-        lax.psum(grad_query.astype(jnp.bfloat16), "dp").astype(jnp.float32),
+        add_all(grad_query.astype(jnp.bfloat16), "dp").astype(jnp.float32),
         lax.psum(grad_out.astype(jnp.bfloat16), "dp").astype(jnp.float32),
         lax.psum(grad_gate.astype(jnp.bfloat16), "dp").astype(jnp.float32),
         lax.psum(grad_up.astype(jnp.bfloat16), "dp").astype(jnp.float32),

time: 763 us -> 849 us (1.11)
  waiting for transfers between devices: 475 us -> 560 us
    all_gather x0 -> x1, waiting for transfers between devices: none -> 135 us  [add_all(): parts = lax.all_gather(x, name, axis=0, tiled=False)]
    psum x1, waiting for transfers between devices: 227 us -> 200 us  [local(): lax.psum(grad_out.astype(jnp.bfloat16), 'dp').astype(jnp.float32)]
    psum x1, waiting for transfers between devices: 168 us -> 146 us  [local(): lax.psum((grad_key, grad_value, grad_attn_in, grad_attn_out, grad_ffn_in,...]
  transfers between devices with their start and end apart: 7 -> 8, of which waited for: 6 -> 7; matrix products, arithmetic and copies ran while one was open for 4% -> 6% of each run, Pallas kernels for 0% -> 0%
where the time goes in v1:
time: 849 us; the launch traced here: 848 us
  waiting for transfers between devices  560 us (66%)
  blocking collectives  128 us (15%)
  matrix products  50.7 us (6%)
  other arithmetic  47.5 us (6%)
  local copies, waits for them, and re-layouts  26.5 us (3%)
  starting transfers between devices  19.9 us (2%)
  between operations  14.6 us (2%)
    psum x1, waiting for transfers between devices, local(): lax.psum(grad_out.astype(jnp.bfloat16), 'dp').astype(jnp.float32)  200 us
    psum x1, waiting for transfers between devices, local(): lax.psum((grad_key, grad_value, grad_attn_in, grad_attn_out, grad_ffn_in,...  146 us
    all_gather x1, waiting for transfers between devices, add_all(): parts = lax.all_gather(x, name, axis=0, tiled=False)  135 us
    psum x1, blocking collectives, local(): lax.psum((grad_key, grad_value, grad_attn_in, grad_attn_out, grad_ffn_in,...  70.1 us
    all_to_all x2, blocking collectives, sum_at_owner(): tiles = lax.all_to_all(in_blocks(x, dim, size), axis, 0, 0, tiled=True)  38.5 us
    all_gather x1, waiting for transfers between devices, in_one_piece(): lax.all_gather(both, axis, axis=dim, tiled=True)  36.8 us
    all_to_all x2, waiting for transfers between devices, sum_at_owner(): tiles = lax.all_to_all(in_blocks(x, dim, size), axis, 0, 0, tiled=True)  33.4 us
    all_to_all x1, blocking collectives, copy_for_each(): return lax.all_to_all(copies, axis, split_axis=0, concat_axis=0, tiled=True)  19.7 us
  transfers between devices with their start and end apart: 8, of which 7 were waited for; matrix products, arithmetic and copies ran while one was open for 6% of the time, Pallas kernels for 0%

profile of v1, /device:TPU:1, one launch (start us, length us, event | category | flops | bytes accessed | tf_op | source)
XLA Modules:
  0.0 847.7 jit_solution(17462549218330773450)
XLA Ops:
  9.8 1.6 multiply_reduce_fusion.1
  11.5 2.1 convolution_convert_fusion.6
  15.7 2.4 fusion.97
  18.3 2.4 fusion.91
  22.7 10.4 %while.28 = (s32[]{:T(128)}, bf16[2,1,512,256]{3,2,1,0:T(8,128)(2,1)S(1)}, f32[2,1,512]{2,1,0:T(1,128)}, s32[2,512]{1,0:T(2,128)S(1)}, s32[2,1024]{1,0:T(2,128)S...) while((s32[]{:T(128)}, ...), condition=%wide.region_6.7_spmd.clone, body=%wide.region_3.6_spmd.sunk.clone | while | flops 552075264 | bytes 8220833 | solution.py:218
  22.7 2.0 fusion.189
  25.8 1.4 fusion.191
  27.9 2.0 fusion.189
  30.9 1.4 fusion.191
  33.0 2.6 convolution_convert_fusion
  35.6 5.7 all-to-all-start
  41.3 1.8 convert_element_type.146
  43.1 14.8 %all-to-all-done = bf16[4,256,640]{2,1,0:T(8,128)(2,1)} async-done(((bf16[4,256,640]{2,1,0:T(8,128)(2,1)}), bf16[4,256,640]{2,1,0:T(8,128)(2,1)}, u32[]{:S(2)}, u32[]{:S(2)}) %all-to-all-start) | async-done | bytes 1310752 | tf_op jit(solution)/shard_map/all_to_all | solution.py:27
  57.8 1.6 convert_reduce_fusion.3
  60.1 2.0 multiply_reduce_fusion.14
  62.9 19.7 %all_to_all.35 = bf16[4,256,640]{2,1,0:T(8,128)(2,1)S(1)} all-to-all(bf16[4,256,640]{2,1,0:T(8,128)(2,1)S(1)} %broadcast_in_dim.57), channel_id=1, replica_groups=mesh['dp'=32,'tensor'=4] {'tensor'}, dimensions={0} | all-to-all | bytes 2621440 | tf_op jit(solution)/shard_map/all_to_all | solution.py:39
  84.1 2.6 multiply_convert_fusion.3
  87.8 19.8 %all_to_all.36 = bf16[4,256,640]{2,1,0:T(8,128)(2,1)S(1)} all-to-all(bf16[4,256,640]{2,1,0:T(8,128)(2,1)S(1)} %bitcast.224), channel_id=1, replica_groups=mesh['dp'=32,'tensor'=4] {'tensor'}, dimensions={0} | all-to-all | bytes 2621440 | tf_op jit(solution)/shard_map/all_to_all | solution.py:27
  110.1 36.8 %all-gather.4.cloned.1.call-done = bf16[1024,1280]{1,0:T(8,128)(2,1)} async-done(((bf16[256,1280]{1,0:T(8,128)(2,1)}), bf16[1024,1280]{1,0:T(8,128)(2,1)}) %all-gather.4.cloned.1.call-update) | async-done | bytes 2621456 | tf_op jit(solution)/shard_map/all_gather | solution.py:48
  146.9 5.0 multiply_convert_fusion.2
  154.6 18.6 %all_to_all.37 = bf16[4,256,640]{2,1,0:T(8,128)(2,1)S(1)} all-to-all(bf16[4,256,640]{2,1,0:T(8,128)(2,1)S(1)} %bitcast.210), channel_id=1, replica_groups=mesh['dp'=32,'tensor'=4] {'tensor'}, dimensions={0} | all-to-all | bytes 2621440 | tf_op jit(solution)/shard_map/all_to_all | solution.py:27
  174.4 2.0 multiply_reduce_fusion.7
  177.7 5.3 all-to-all-start.4
  183.0 3.0 convolution_convert_fusion.3
  186.1 1.7 convolution_convert_fusion.4
  188.3 1.9 convolution_convert_fusion.2
  190.2 9.3 %all-to-all-done.4 = bf16[4,256,640]{2,1,0:T(8,128)(2,1)} async-done(((bf16[4,256,640]{2,1,0:T(8,128)(2,1)}), bf16[4,256,640]{2,1,0:T(8,128)(2,1)}, u32[]{:S(2)}, u32[]{:S(2)}) %all-to-all-start.4) | async-done | bytes 1310752 | tf_op jit(solution)/shard_map/all_to_all | solution.py:39
  199.5 2.6 convolution_convert_fusion.7
  202.2 2.1 convolution_convert_fusion.5
  204.6 15.3 %while.29 = (s32[]{:T(128)}, f32[2,1,512,256]{3,2,1,0:T(8,128)S(1)}, f32[2,1024,256]{2,1,0:T(8,128)}, f32[2,1024,256]{2,1,0:T(8,128)}, s32[2,512]{1,0:T(2,128)S(...) while((s32[]{:T(128)}, ...), condition=%wide.region_18.19_spmd.clone, body=%wide.region_16.18_spmd.sunk.clone | while | flops 1349910528 | bytes 58758412 | solution.py:269
  220.0 2.3 fusion.94
  223.6 1.5 convolution_convert_fusion.8
  227.3 1.4 slice_add_fusion.1
  228.8 2.3 fusion.100
  234.7 1.7 add_convert_fusion
  236.4 4.5 all-to-all-start.5
  240.9 18.7 %all-to-all-done.5 = bf16[4,256,640]{2,1,0:T(8,128)(2,1)S(1)} async-done(((bf16[4,256,640]{2,1,0:T(8,128)(2,1)}), bf16[4,256,640]{2,1,0:T(8,128)(2,1)S(1)}, u32[]{:S(2)}, u32[]{:S(2)}) %all-to-all-start.5) | async-done | bytes 1310752 | tf_op jit(solution)/shard_map/all_to_all | solution.py:27
  263.5 4.2 all-to-all-start.6
  267.7 2.6 fusion.113
  270.3 1.6 fusion.112
  271.9 2.5 slice.62
  274.4 70.1 %all-reduce.9 = (f32[640]{0:T(1024)}, f32[640]{0:T(1024)}, f32[640]{0:T(1024)}, f32[640]{0:T(1024)}, f32[256]{0:T(256)}, /*index=5*/f32[256]{0:T(256)}) all-reduce(f32[640]{0:T(1024)S(1)} %get-tuple-element.133, f32[640]{0:T(1024)S(1)} %copy-done.59, f32[640]{0:T(1024)S(1)} %copy-done.58, ...), channel_id=1, replica_groups=mesh['dp'=32,'tensor'=4] {'dp','tensor'}, use_global_device_ids=true, to_apply=%region_32.33 | all-reduce | flops 3072 | bytes 24576 | tf_op jit(solution)/shard_map/psum | solution.py:315
  344.5 200.2 %all-reduce.17.cloned.1.call-done = (bf16[256,640]{1,0:T(8,128)(2,1)}, bf16[640,512]{1,0:T(8,128)(2,1)}, bf16[640,512]{1,0:T(8,128)(2,1)}, bf16[512,640]{1,0:T(8,128)(2,1)}) async-done(((bf16[256,640]{1,0:T(8,128)(2,1)}, bf16[640,512]{1,0:T(8,128)(2,1)}, bf16[640,512]{1,0:T(8,128)(2,1)}, bf16[512,640]{1,0:T(8,128)(2,1)}), (bf16[256,640]{1,0:T(8,128)(2,1)}, bf16[640,512]{1,0:T(8,128)(2,1)}, ...) | async-done | bytes 2293776 | tf_op jit(solution)/shard_map/psum | solution.py:310
  544.7 1.9 convert_element_type.177
  546.6 2.4 convert_element_type.179
  551.4 134.5 %all-gather.6.cloned.1.call-done = bf16[20480,256]{1,0:T(8,128)(2,1)} async-done(((bf16[640,256]{1,0:T(8,128)(2,1)}), bf16[20480,256]{1,0:T(8,128)(2,1)}) %all-gather.6.cloned.1.call-update) | async-done | bytes 10485776 | tf_op jit(solution)/shard_map/all_gather | solution.py:15
  685.9 5.7 reduce_sum.263
  692.4 145.5 %all-reduce.15.cloned.1.call-done = (f32[640,256]{1,0:T(8,128)}, f32[640,256]{1,0:T(8,128)}) async-done(((f32[640,256]{1,0:T(8,128)}, f32[640,256]{1,0:T(8,128)}), (f32[640,256]{1,0:T(8,128)}, f32[640,256]{1,0:T(8,128)})) %all-reduce.15.cloned.1.call-update) | async-done | bytes 1310736 | tf_op jit(solution)/shard_map/psum | solution.py:315
  (282 shorter events, 55.0 us)
Async XLA Ops:
  7.2 79.6 %copy-start = (bf16[512,640]{1,0:T(8,128)(2,1)S(1)}, bf16[512,640]{1,0:T(8,128)(2,1)}, u32[]{:S(2)}) copy-start(bf16[512,640]{1,0:T(8,128)(2,1)} %param.31) | copy-start | bytes 1966084
  11.5 3.0 copy-start.75
  15.4 2.7 copy-start.62
  15.4 2.9 copy-start.4
  15.4 2.7 copy-start.64
  15.4 2.7 copy-start.42
  35.6 22.2 %all-to-all-start = ((bf16[4,256,640]{2,1,0:T(8,128)(2,1)}), bf16[4,256,640]{2,1,0:T(8,128)(2,1)}, u32[]{:S(2)}, u32[]{:S(2)}) async-start(bf16[4,256,640]{2,1,0:T(8,128)(2,1)} %bitcast.29), calls=%async_computation | async-start | bytes 2621440 | tf_op jit(solution)/shard_map/all_to_all | solution.py:27
  41.3 105.6 %all-gather.4.cloned.1.call-start = ((), (), s32[]{:S(2)}) async-start(), calls=%async_computation.7 | async-start | bytes 3276800 | tf_op jit(solution)/shard_map/all_gather | solution.py:48
  57.8 4.8 copy-start.44
  62.8 19.8 %copy-start.30 = (bf16[640,512]{1,0:T(8,128)(2,1)S(1)}, bf16[640,512]{1,0:T(8,128)(2,1)}, u32[]{:S(2)}) copy-start(bf16[640,512]{1,0:T(8,128)(2,1)} %param.29) | copy-start | bytes 1966084
  84.1 2.6 copy-start.77
  86.8 20.9 %copy-start.78 = (bf16[1024,512]{1,0:T(8,128)(2,1)}, bf16[1024,512]{1,0:T(8,128)(2,1)S(1)}, u32[]{:S(2)}) copy-start(bf16[1024,512]{1,0:T(8,128)(2,1)S(1)} %get-tuple-element.219) | copy-start | bytes 3145732
  87.8 20.2 %copy-start.24 = (bf16[1024,640]{1,0:T(8,128)(2,1)S(1)}, bf16[1024,640]{1,0:T(8,128)(2,1)}, u32[]{:S(2)}) copy-start(bf16[1024,640]{1,0:T(8,128)(2,1)} %param.24) | copy-start | bytes 3932164
  87.8 20.2 %copy-start.54 = (f32[640]{0:T(1024)S(1)}, f32[640]{0:T(1024)}, u32[]{:S(2)}) copy-start(f32[640]{0:T(1024)} %param.35) | copy-start | bytes 7684
  146.9 5.1 copy-start.31
  154.6 18.9 %copy-start.45 = (f32[640]{0:T(1024)S(1)}, f32[640]{0:T(1024)}, u32[]{:S(2)}) copy-start(f32[640]{0:T(1024)} %param.34) | copy-start | bytes 7684
  154.6 18.9 %copy-start.53 = (f32[256]{0:T(256)S(1)}, f32[256]{0:T(256)}, u32[]{:S(2)}) copy-start(f32[256]{0:T(256)} %copy-done.52) | copy-start | bytes 3076
  173.5 2.9 copy-start.70
  176.6 6.5 copy-start.13
  177.7 21.8 %all-to-all-start.4 = ((bf16[4,256,640]{2,1,0:T(8,128)(2,1)}), bf16[4,256,640]{2,1,0:T(8,128)(2,1)}, u32[]{:S(2)}, u32[]{:S(2)}) async-start(bf16[4,256,640]{2,1,0:T(8,128)(2,1)} %broadcast_in_dim.61), calls=%async_computation.4 | async-start | bytes 2621440 | tf_op jit(solution)/shard_map/all_to_all | solution.py:39
  183.0 361.6 %all-reduce.17.cloned.1.call-start = ((), (), s32[]{:S(2)}) async-start(), calls=%async_computation.10 | async-start | bytes 4587520 | tf_op jit(solution)/shard_map/psum | solution.py:310
  183.0 3.0 copy-start.22
  202.2 2.4 copy-start.19
  202.2 2.4 copy-start.34
  202.2 2.4 copy-start.49
  204.3 481.6 %all-gather.6.cloned.1.call-start = ((), (), s32[]{:S(2)}) async-start(), calls=%async_computation.8 | async-start | bytes 10813440 | tf_op jit(solution)/shard_map/all_gather | solution.py:15
  204.6 15.4 %copy-start.74 = (f32[128]{0:T(128)S(1)}, f32[128]{0:T(128)}, u32[]{:S(2)}) copy-start(f32[128]{0:T(128)} %multiply_power_fusion) | copy-start | bytes 1540
  219.9 2.3 copy-start.43
  219.9 2.3 copy-start.65
  220.0 2.8 copy-start.63
  227.3 3.8 copy-start.3
  227.3 3.8 copy-start.41
  227.3 3.8 copy-start.67
  228.8 2.8 copy-start.61
  228.8 2.8 copy-start.16
  236.4 4.5 copy-start.68
  236.4 23.2 %all-to-all-start.5 = ((bf16[4,256,640]{2,1,0:T(8,128)(2,1)}), bf16[4,256,640]{2,1,0:T(8,128)(2,1)S(1)}, u32[]{:S(2)}, u32[]{:S(2)}) async-start(bf16[4,256,640]{2,1,0:T(8,128)(2,1)} %bitcast.44), calls=%async_computation.5 | async-start | bytes 2621440 | tf_op jit(solution)/shard_map/all_to_all | solution.py:27
  240.9 20.1 %copy-start.7 = (f32[256,640]{1,0:T(8,128)S(1)}, f32[256,640]{1,0:T(8,128)}, u32[]{:S(2)}) copy-start(f32[256,640]{1,0:T(8,128)} %copy-done.6) | copy-start | bytes 1966084
  262.3 5.4 copy-start.10
  263.5 81.0 %all-to-all-start.6 = ((bf16[4,256,640]{2,1,0:T(8,128)(2,1)}), bf16[4,256,640]{2,1,0:T(8,128)(2,1)S(1)}, u32[]{:S(2)}, u32[]{:S(2)}) async-start(bf16[4,256,640]{2,1,0:T(8,128)(2,1)} %broadcast_in_dim.101), calls=%async_computation.6 | async-start | bytes 2621440 | tf_op jit(solution)/shard_map/all_to_all | solution.py:39
  267.7 570.3 %all-reduce.15.cloned.1.call-start = ((), (), s32[]{:S(2)}) async-start(), calls=%async_computation.9 | async-start | bytes 2621440 | tf_op jit(solution)/shard_map/psum | solution.py:315
  271.9 2.5 copy-start.57
  271.9 2.5 copy-start.58
  271.9 2.5 copy-start.59
  544.7 4.3 copy-start.29
  546.6 3.6 copy-start.28
  837.9 2.4 copy-start.26
  837.9 3.2 copy-start.1
  (47 other events, 63.4 us)
Sparse Core Ops, SparseCore 0:
  110.2 36.6 all-gather.3
  204.4 340.2 all-reduce.16
  548.4 137.4 all-gather.5
  691.3 146.6 all-reduce.14
